TPU v7x, 32 devices: a whole 2x2x4 slice. The times are simulated.
32 devices in a mesh: group: 2 (over x), expert: 4 (over y, core), dp: 4 (over z).
Axes of the slice: x: 2, y: 2, z: 4, core: 2. Of those that a mesh axis runs over, the one named last changes fastest.
Arguments:
- query: bfloat16 [256, 8192], P(('group', 'expert', 'dp')), parts along dimension 0, may hold values from -5 to 5
- key_cache: bfloat16 [256, 4, 256, 128], P(('group', 'expert', 'dp')), parts along dimension 0, may hold values from -5 to 5
- value_cache: bfloat16 [256, 4, 256, 128], P(('group', 'expert', 'dp')), parts along dimension 0, may hold values from -6 to 6
- new_key: bfloat16 [256, 512], P(('group', 'expert', 'dp')), parts along dimension 0, may hold values from -5 to 5
- new_value: bfloat16 [256, 512], P(('group', 'expert', 'dp')), parts along dimension 0, may hold values from -6 to 6
- lengths: int32 [256], P(('group', 'expert', 'dp')), parts along dimension 0, may hold values from 2 to 256, as said below
- residual: bfloat16 [256, 4096], P(('group', 'expert', 'dp')), parts along dimension 0, may hold values from -4 to 4
- out_proj: bfloat16 [8192, 4096], P('expert'), may hold values from -0.5 to 0.5
- norm_gain: float32 [4096], replicated, may hold values from 0.5 to 1.5
- expert_ids: int32 [256, 8], P(('group', 'expert', 'dp')), parts along dimension 0, may hold values from 0 to 15, all different within a row; in each aligned block of 8 rows (0 to 7, 8 to 15, ...) at most 6 rows name the same one
- gate_probs: float32 [256, 8], P(('group', 'expert', 'dp')), parts along dimension 0, may hold values from 0.02 to 1
- w_gate: bfloat16 [16, 4096, 1536], P('expert', None, 'dp'), may hold values from -0.09375 to 0.09375
- w_up: bfloat16 [16, 4096, 1536], P('expert', None, 'dp'), may hold values from -0.09375 to 0.09375
- w_down: bfloat16 [16, 1536, 4096], P('expert', 'dp'), may hold values from -0.625 to 0.625
Outputs:
- layer_out: bfloat16 [256, 4096], P(('group', 'expert', 'dp')), parts along dimension 0
There are 2 independent parts, one for each index of `group`. A program takes and returns all parts, laid end to end along the dimension named above; an argument that names none is the same for every part. Nothing has to cross between parts.
Inputs may be any that keep to these rules, and one draw needn't show every extreme that they name: `lengths`: some row holds 256 cached positions. `expert_ids`: each row names 8 different experts; among the rows of one device no expert is named by more than 6 rows.
All inputs are finite; a program needn't handle non-finite values.
Results may differ from a plain program's by a relative error of at most 0.0074.
Values may be sent and summed in bfloat16 or wider, within the bound.
A program may use at most 128 MiB of HBM per device.

v0:
```python
import math

import jax
import jax.numpy as jnp
from jax import lax
from jax.sharding import PartitionSpec as P

EPS = 1e-06


def attend(query, key_cache, value_cache, new_key, new_value, lengths):
    row_count = query.shape[0]
    kv_count = key_cache.shape[1]
    cache_len = key_cache.shape[2]
    head_size = key_cache.shape[3]
    per_group = query.shape[1] // (kv_count * head_size)
    queries = query.reshape(row_count, kv_count, per_group, head_size)
    scaling = 1.0 / math.sqrt(head_size)
    scores = (
        jnp.einsum("rkgd,rkcd->rkgc", queries, key_cache, preferred_element_type=jnp.float32)
        * scaling
    )
    fresh_keys = new_key.reshape(row_count, kv_count, head_size)
    self_score = (
        jnp.einsum("rkgd,rkd->rkg", queries, fresh_keys, preferred_element_type=jnp.float32)
        * scaling
    )
    usable = jnp.arange(cache_len, dtype=jnp.int32)[None, :] < lengths[:, None]
    scores = jnp.where(usable[:, None, None, :], scores, -jnp.inf)
    highest = jnp.maximum(jnp.max(scores, axis=-1), self_score)
    exponent = jnp.exp(scores - highest[..., None])
    self_exp = jnp.exp(self_score - highest)
    denominator = jnp.sum(exponent, axis=-1) + self_exp
    weights = (exponent / denominator[..., None]).astype(jnp.bfloat16)
    self_weight = lax.optimization_barrier((self_exp / denominator).astype(jnp.bfloat16)).astype(
        jnp.float32
    )
    fresh_values = new_value.astype(jnp.float32).reshape(row_count, kv_count, head_size)
    attended = jnp.einsum(
        "rkgc,rkcd->rkgd", weights, value_cache, preferred_element_type=jnp.float32
    )
    attended = attended + self_weight[..., None] * fresh_values[:, :, None, :]
    return attended.astype(jnp.bfloat16).reshape(row_count, per_group * kv_count * head_size)


def routing(expert_ids, gate_probs, expert_total):
    normalized = gate_probs / jnp.sum(gate_probs, axis=-1, keepdims=True)
    matches = expert_ids[:, :, None] == jnp.arange(expert_total, dtype=jnp.int32)[None, None, :]
    return jnp.sum(jnp.where(matches, normalized[:, :, None], 0.0), axis=1).astype(jnp.bfloat16)


def expert_apply(row_block, weight_block, w_gate, w_up):
    gate_out = jnp.einsum("md,kdf->mkf", row_block, w_gate, preferred_element_type=jnp.float32)
    up_out = jnp.einsum("md,kdf->mkf", row_block, w_up, preferred_element_type=jnp.float32)
    activated = (
        jax.nn.silu(gate_out) * up_out * weight_block.astype(jnp.float32)[:, :, None]
    ).astype(jnp.bfloat16)
    return activated.reshape(row_block.shape[0], -1)


def per_device(
    query,
    key_cache,
    value_cache,
    new_key,
    new_value,
    lengths,
    residual,
    out_proj,
    norm_gain,
    expert_ids,
    gate_probs,
    w_gate,
    w_up,
    w_down,
):
    width = residual.shape[1]
    local_experts = w_gate.shape[0]
    n_expert = lax.axis_size("expert")
    down_flat = w_down.reshape(-1, width)
    attended = attend(query, key_cache, value_cache, new_key, new_value, lengths)
    received = lax.all_to_all(attended, "expert", split_axis=1, concat_axis=0, tiled=True)
    projected = lax.psum_scatter(
        jnp.dot(received, out_proj, preferred_element_type=jnp.float32),
        "expert",
        scatter_dimension=0,
        tiled=True,
    )
    hidden = (residual.astype(jnp.float32) + projected).astype(jnp.bfloat16)
    hidden_wide = hidden.astype(jnp.float32)
    mean_square = jnp.mean(hidden_wide * hidden_wide, axis=-1, keepdims=True)
    normed = (hidden_wide * lax.rsqrt(mean_square + EPS) * norm_gain).astype(jnp.bfloat16)
    expert_total = local_experts * n_expert
    weighting = routing(expert_ids, gate_probs, expert_total)
    all_rows, all_weighting = (
        lax.all_gather(normed, ("expert", "dp"), axis=0, tiled=True),
        lax.all_gather(weighting, ("expert", "dp"), axis=0, tiled=True),
    )
    first_expert = lax.axis_index("expert") * local_experts
    local_weighting = lax.dynamic_slice_in_dim(all_weighting, first_expert, local_experts, 1)
    activated = expert_apply(all_rows, local_weighting, w_gate, w_up)
    expert_sum = lax.psum_scatter(
        jnp.dot(activated, down_flat, preferred_element_type=jnp.float32),
        ("expert", "dp"),
        scatter_dimension=0,
        tiled=True,
    )
    return (hidden_wide + expert_sum).astype(jnp.bfloat16)


def solution(mesh):
    return jax.shard_map(
        per_device,
        mesh=mesh,
        in_specs=(
            P(("group", "expert", "dp"), None),
            P(("group", "expert", "dp"), None, None, None),
            P(("group", "expert", "dp"), None, None, None),
            P(("group", "expert", "dp"), None),
            P(("group", "expert", "dp"), None),
            P(("group", "expert", "dp")),
            P(("group", "expert", "dp"), None),
            P("expert", None),
            P(),
            P(("group", "expert", "dp"), None),
            P(("group", "expert", "dp"), None),
            P("expert", None, "dp"),
            P("expert", None, "dp"),
            P("expert", "dp", None),
        ),
        out_specs=P(("group", "expert", "dp"), None),
        check_vma=False,
    )
```

profile of v0, /device:TPU:0, one launch (start us, length us, event | category | flops | bytes accessed | tf_op | source)
XLA Modules:
  0.0 184.2 jit_solution(3972106118809428674)
XLA Ops:
  6.5 0.9 iota_compare_fusion.1
  7.4 0.7 bitcast_convert_fusion
  8.1 1.1 fusion.16
  9.2 1.6 fusion.21
  10.9 0.3 fusion.7
  11.2 2.1 %fusion.3 = bf16[8,4,16,128]{3,2,1,0:T(8,128)(2,1)S(1)} fusion(bf16[8,4,256,128]{3,2,1,0:T(8,128)(2,1)} %param.16, f32[8,4,16,256]{3,2,1,0:T(8,128)S(1)} %get-tuple-element.10, f32[8,4,16]{2,1,0:T(4,128)S(1)} %get-tuple-element.8, f32[8,4,16]{2,1,0:T(4,128)S(1)} %multiply_maximum_fusion, f32[8,4,128]{2,1,0:T(4,128)S(1)} %copy.29, ...), kind=kOutput, calls=%fused_computation.7 | convolution fusion | flops 34144256 | bytes 2775040 | tf_op jit(solution)/shard_map/rkgc,rkcd->rkgd/dot_general | solution.py:39
  13.3 0.0 copy-start.2
  13.3 0.0 copy-start.3
  13.3 0.1 copy.30
  13.4 0.0 copy-start.4
  13.4 0.0 copy-start.5
  13.5 8.7 %all_to_all.19 = bf16[8,4,2048]{2,0,1:T(8,128)(2,1)S(1)} all-to-all(bf16[8,4,2048]{2,0,1:T(8,128)(2,1)S(1)} %copy.30), channel_id=1, replica_groups=mesh['group'=2,'expert'=4,'dp'=4] {'expert'}, dimensions={1} | all-to-all | bytes 262144 | tf_op jit(solution)/shard_map/all_to_all | solution.py:82
  22.1 9.5 %fusion.14 = f32[32,4096]{1,0:T(8,128)} fusion(bf16[2048,4096]{1,0:T(8,128)(2,1)} %param.21, bf16[8,4,2048]{2,0,1:T(8,128)(2,1)S(1)} %all_to_all.19), kind=kOutput, calls=%fused_computation.23 | convolution fusion | flops 536870912 | bytes 17432576 | tf_op jit(solution)/shard_map/dot_general | solution.py:84
  31.7 0.0 reduce-scatter.3.cloned.1.call-update
  31.7 0.0 all-gather.2.cloned.1.call-start
  31.7 22.1 %reduce-scatter.3.cloned.1.call-done = f32[8,4096]{1,0:T(8,128)} async-done(((f32[32,4096]{1,0:T(8,128)}), f32[8,4096]{1,0:T(8,128)}) %reduce-scatter.3.cloned.1.call-update) | async-done | bytes 131088 | tf_op jit(solution)/shard_map/reduce_scatter | solution.py:83
  53.8 1.1 fusion.10
  54.9 0.7 fusion.12
  55.6 0.0 all-gather.2.cloned.1.call-update
  55.6 0.0 reduce-scatter.5.cloned.1.call-start
  55.7 0.1 reduce_sum.38
  55.8 0.1 broadcast_divide_fusion
  55.9 0.1 select_reduce_fusion
  56.0 31.5 %all_gather.7 = bf16[128,16]{1,0:T(8,128)(2,1)S(1)} all-gather(bf16[8,16]{1,0:T(8,128)(2,1)S(1)} %select_reduce_fusion), channel_id=1, replica_groups=mesh['group'=2,'expert'=4,'dp'=4] {'expert','dp'}, dimensions={0}, use_global_device_ids=true | all-gather | bytes 4352 | tf_op jit(solution)/shard_map/all_gather | solution.py:97
  87.5 0.1 constant_dynamic-slice_fusion
  87.6 0.1 copy.34
  87.7 6.5 %all-gather.2.cloned.1.call-done = bf16[128,4096]{1,0:T(8,128)(2,1)} async-done(((bf16[8,4096]{1,0:T(8,128)(2,1)}), bf16[128,4096]{1,0:T(8,128)(2,1)}) %all-gather.2.cloned.1.call-update) | async-done | bytes 1048592 | tf_op jit(solution)/shard_map/all_gather | solution.py:96
  94.2 7.7 %fusion.5 = f32[128,4,384]{2,0,1:T(8,128)} fusion(bf16[4,4096,384]{2,1,0:T(8,128)(2,1)} %param.25, bf16[128,4096]{1,0:T(8,128)(2,1)} %all-gather.2.cloned.1.call-done), kind=kOutput, calls=%fused_computation.9 | convolution fusion | flops 1610612736 | bytes 14417920 | tf_op jit(solution)/shard_map/md,kdf->mkf/dot_general | solution.py:53
  101.9 13.4 %convolution_bitcast_fusion = f32[128,4096]{1,0:T(8,128)} fusion(bf16[4,384,4096]{2,1,0:T(8,128)(2,1)} %param.27, bf16[4,4096,384]{2,1,0:T(8,128)(2,1)} %param.26, bf16[128,4096]{1,0:T(8,128)(2,1)S(1)} %copy-done.1, f32[128,4,384]{2,0,1:T(8,128)} %fusion.5, f32[128,4]{0,1:T(4,128)S(1)} %convert_element_type.46), kind=kOutput, calls=%fused_computation | convolution fusion | flops 3222601728 | bytes 29100032 | tf_op jit(solution)/shard_map/dot_general | solution.py:103
  115.4 0.0 reduce-scatter.5.cloned.1.call-update
  115.4 60.7 %reduce-scatter.5.cloned.1.call-done = f32[8,4096]{1,0:T(8,128)} async-done(((f32[128,4096]{1,0:T(8,128)}), f32[8,4096]{1,0:T(8,128)}) %reduce-scatter.5.cloned.1.call-update) | async-done | bytes 131088 | tf_op jit(solution)/shard_map/reduce_scatter | solution.py:102
  176.1 1.5 fusion.13
  (16 shorter events, 0.1 us)
Async XLA Ops:
  6.5 2.7 %copy-start = (bf16[8,4,256,128]{3,2,1,0:T(8,128)(2,1)S(1)}, bf16[8,4,256,128]{3,2,1,0:T(8,128)(2,1)}, u32[]{:S(2)}) copy-start(bf16[8,4,256,128]{3,2,1,0:T(8,128)(2,1)} %param.15) | copy-start | bytes 6291460
  6.5 47.3 %reduce-scatter.3.cloned.1.call-start = ((), (), s32[]{:S(2)}) async-start(), calls=%async_computation.3 | async-start | bytes 655360 | tf_op jit(solution)/shard_map/reduce_scatter | solution.py:83
  13.3 40.6 %copy-start.2 = (bf16[8,4096]{1,0:T(8,128)(2,1)S(1)}, bf16[8,4096]{1,0:T(8,128)(2,1)}, u32[]{:S(2)}) copy-start(bf16[8,4096]{1,0:T(8,128)(2,1)} %param.20) | copy-start | bytes 196612
  13.3 41.6 %copy-start.3 = (f32[4096]{0:T(1024)S(1)}, f32[4096]{0:T(1024)}, u32[]{:S(2)}) copy-start(f32[4096]{0:T(1024)} %param.22) | copy-start | bytes 49156
  13.4 42.3 %copy-start.4 = (f32[8,8]{1,0:T(8,128)S(1)}, f32[8,8]{1,0:T(8,128)}, u32[]{:S(2)}) copy-start(f32[8,8]{1,0:T(8,128)} %param.24) | copy-start | bytes 772
  13.4 42.5 %copy-start.5 = (s32[8,8]{1,0:T(8,128)S(1)}, s32[8,8]{1,0:T(8,128)}, u32[]{:S(2)}) copy-start(s32[8,8]{1,0:T(8,128)} %param.23) | copy-start | bytes 772
  31.7 62.5 %all-gather.2.cloned.1.call-start = ((), (), s32[]{:S(2)}) async-start(), calls=%async_computation.4 | async-start | bytes 1114112 | tf_op jit(solution)/shard_map/all_gather | solution.py:96
  55.6 120.4 %reduce-scatter.5.cloned.1.call-start = ((), (), s32[]{:S(2)}) async-start(), calls=%async_computation.5 | async-start | bytes 2228224 | tf_op jit(solution)/shard_map/reduce_scatter | solution.py:102
  94.2 7.7 %copy-start.1 = (bf16[128,4096]{1,0:T(8,128)(2,1)S(1)}, bf16[128,4096]{1,0:T(8,128)(2,1)}, u32[]{:S(2)}) copy-start(bf16[128,4096]{1,0:T(8,128)(2,1)} %all-gather.2.cloned.1.call-done) | copy-start | bytes 3145732
Sparse Core Ops, SparseCore 0:
  31.8 21.9 reduce-scatter.2
  56.3 37.9 all-gather.1
  115.5 60.5 reduce-scatter.4
where the time goes:
time: 185 us; the launch traced here: 184 us
  waiting for transfers between devices  89.4 us (48%)
  blocking collectives  40.2 us (22%)
  matrix products  35.4 us (19%)
  between operations  13.2 us (7%)
  other arithmetic  5.52 us (3%)
    reduce_scatter x1, waiting for transfers between devices, per_device(): lax.psum_scatter(jnp.dot(activated, down_flat, preferred_element_type=jnp...  60.7 us
    all_gather x1, blocking collectives, per_device(): lax.all_gather(weighting, ('expert', 'dp'), axis=0, tiled=True)  31.5 us
    reduce_scatter x1, waiting for transfers between devices, per_device(): lax.psum_scatter(jnp.dot(received, out_proj, preferred_element_type=jnp.f...  22.1 us
    dot_general x1, matrix products, per_device(): jnp.dot(activated, down_flat, preferred_element_type=jnp.float32)  13.4 us
    dot_general x1, matrix products, per_device(): jnp.dot(received, out_proj, preferred_element_type=jnp.float32)  9.55 us
    all_to_all x1, blocking collectives, per_device(): lax.all_to_all(attended, 'expert', split_axis=1, concat_axis=0, tiled=True)  8.67 us
    dot_general x1, matrix products, expert_apply(): jnp.einsum('md,kdf->mkf', row_block, w_gate, preferred_element_type=jnp.f...  7.69 us
    all_gather x1, waiting for transfers between devices, per_device(): lax.all_gather(normed, ('expert', 'dp'), axis=0, tiled=True)  6.54 us
  transfers between devices with their start and end apart: 3, of which 3 were waited for; matrix products, arithmetic and copies ran while one was open for 0% of the time, Pallas kernels for 0%

commit v1 on v0

--- a/solution.py
+++ b/solution.py
@@ -1,8 +1,11 @@
+import functools
 import math
 
 import jax
 import jax.numpy as jnp
 from jax import lax
+from jax.experimental import pallas as pl
+from jax.experimental.pallas import tpu as pltpu
 from jax.sharding import PartitionSpec as P
 
 EPS = 1e-06
@@ -108,9 +111,470 @@
     return (hidden_wide + expert_sum).astype(jnp.bfloat16)
 
 
+MESH = pl.DeviceIdType.MESH
+F32 = jnp.float32
+BF16 = jnp.bfloat16
+CHUNKS = 4
+SIDE = 128
+MIB = 1 << 20
+
+
+def fused_kernel(
+    n_expert,
+    n_dp,
+    query,
+    key_cache,
+    value_cache,
+    new_key,
+    new_value,
+    lengths,
+    residual,
+    out_proj,
+    norm_gain,
+    expert_ids,
+    gate_probs,
+    w_gate,
+    w_up,
+    w_down,
+    out,
+    k_buf,
+    v_buf,
+    wo_buf,
+    gu_buf,
+    q_rows,
+    o_rows,
+    att_send,
+    att_recv,
+    proj_send,
+    proj_recv,
+    proj_own,
+    hidden_buf,
+    gathered,
+    acts,
+    part,
+    s1,
+    r1,
+    s2,
+    r2,
+    s3,
+    r3,
+    kv_sem,
+    wo_sem,
+    gu_sem,
+    wd_sem,
+    att_ssem,
+    att_rsem,
+    proj_ssem,
+    proj_rsem,
+    gat_ssem,
+    gat_rsem,
+    s1_sem,
+    r1_sem,
+    s2_sem,
+    r2_sem,
+    s3_sem,
+    r3_sem,
+):
+    rows, kv_count, cache_len, head_size = key_cache.shape
+    per_group = query.shape[1] // (kv_count * head_size)
+    width = residual.shape[1]
+    feat = att_send.shape[2]
+    local_experts, _, ff = w_gate.shape
+    chunk = width // CHUNKS
+    e = lax.axis_index("expert")
+    z = lax.axis_index("dp")
+    core = lax.rem(e, 2)
+    y = lax.div(e, 2)
+    mate = e + 1 - 2 * core
+    across = lax.rem(e + 2, 4)
+
+    barrier = pltpu.get_barrier_semaphore()
+    for step in range(1, n_expert):
+        pl.semaphore_signal(
+            barrier, inc=1, device_id={"expert": lax.rem(e + step, n_expert)}, device_id_type=MESH
+        )
+    for step in range(1, n_dp):
+        pl.semaphore_signal(
+            barrier, inc=1, device_id={"dp": lax.rem(z + step, n_dp)}, device_id_type=MESH
+        )
+
+    heads = [lax.rem(e + 1 + step, n_expert) for step in range(n_expert)]
+    kv_copies = []
+    for step, k in enumerate(heads):
+        kc = pltpu.make_async_copy(key_cache.at[:, k], k_buf.at[step], kv_sem.at[0, step])
+        vc = pltpu.make_async_copy(value_cache.at[:, k], v_buf.at[step], kv_sem.at[1, step])
+        kc.start()
+        vc.start()
+        kv_copies.append((kc, vc))
+    wo_copies = []
+    for n in range(CHUNKS):
+        cols = pl.ds(n * chunk, chunk)
+        wc = pltpu.make_async_copy(out_proj.at[:, cols], wo_buf.at[:, cols], wo_sem.at[n])
+        wc.start()
+        wo_copies.append(wc)
+    gu_copies = []
+    for j in range(local_experts):
+        for t, w in enumerate((w_gate, w_up)):
+            gc = pltpu.make_async_copy(
+                w.at[j], gu_buf.at[:, pl.ds((2 * j + t) * ff, ff)], gu_sem.at[j, t]
+            )
+            gc.start()
+            gu_copies.append(gc)
+
+    for h in range(kv_count * per_group):
+        q_rows[pl.ds(h, rows, stride=kv_count * per_group), :] = query[
+            :, h * head_size : (h + 1) * head_size
+        ].astype(F32)
+    scaling = 1.0 / math.sqrt(head_size)
+    place = lax.broadcasted_iota(jnp.int32, (per_group, cache_len), 1)
+
+    att_copies = []
+    for step, k in enumerate(heads):
+        kv_copies[step][0].wait()
+        lanes = pl.ds(pl.multiple_of(k * head_size, head_size), head_size)
+        fresh_k = new_key[:, lanes].astype(F32)
+        fresh_v = new_value[:, lanes].astype(F32)
+        scores, selfs = [], []
+        for r in range(rows):
+            start = pl.multiple_of(r * kv_count * per_group + k * per_group, per_group)
+            q = q_rows[pl.ds(start, per_group), :]
+            score = lax.dot_general(
+                q.astype(BF16),
+                k_buf[step, r],
+                (((1,), (1,)), ((), ())),
+                preferred_element_type=F32,
+            )
+            score = jnp.where(place < lengths[r], score * scaling, -jnp.inf)
+            scores.append(score)
+            selfs.append(jnp.sum(q * fresh_k[r : r + 1], axis=-1, keepdims=True) * scaling)
+        score = jnp.concatenate(scores, axis=0)
+        self_score = jnp.concatenate(selfs, axis=0)
+        highest = jnp.maximum(jnp.max(score, axis=-1, keepdims=True), self_score)
+        exponent = jnp.exp(score - highest)
+        self_exp = jnp.exp(self_score - highest)
+        denominator = jnp.sum(exponent, axis=-1, keepdims=True) + self_exp
+        weights = (exponent / denominator).astype(BF16)
+        self_weight = (self_exp / denominator).astype(BF16).astype(F32)
+        kv_copies[step][1].wait()
+        for r in range(rows):
+            band = slice(r * per_group, (r + 1) * per_group)
+            o_rows[band, :] = (
+                jnp.dot(weights[band], v_buf[step, r], preferred_element_type=F32)
+                + self_weight[band] * fresh_v[r : r + 1]
+            )
+        if step == 0:
+            pl.semaphore_wait(barrier, n_expert + n_dp - 2)
+        last = step == n_expert - 1
+        target = att_recv.at[e] if last else att_send.at[step]
+        for h in range(per_group):
+            target[:, h * head_size : (h + 1) * head_size] = o_rows[
+                pl.ds(h, rows, stride=per_group), :
+            ].astype(BF16)
+        if not last:
+            copy = pltpu.make_async_remote_copy(
+                src_ref=att_send.at[step],
+                dst_ref=att_recv.at[e],
+                send_sem=att_ssem.at[step],
+                recv_sem=att_rsem.at[e],
+                device_id={"expert": k},
+                device_id_type=MESH,
+            )
+            copy.start()
+            att_copies.append(copy)
+
+    probs = gate_probs[...]
+    probs = probs / jnp.sum(probs, axis=-1, keepdims=True)
+    ids = expert_ids[...]
+    side_place = lax.broadcasted_iota(jnp.int32, (rows, SIDE), 1)
+    weighting = jnp.zeros((rows, SIDE), F32)
+    for t in range(ids.shape[1]):
+        weighting = weighting + jnp.where(side_place == ids[:, t : t + 1], probs[:, t : t + 1], 0.0)
+    mine = e * n_dp + z
+    gathered[mine, :, width:] = weighting.astype(BF16)
+
+    for step in range(n_expert - 1):
+        src = lax.rem(e + 1 + step, n_expert)
+        pltpu.make_async_remote_copy(
+            src_ref=att_send.at[step],
+            dst_ref=att_recv.at[src],
+            send_sem=att_ssem.at[step],
+            recv_sem=att_rsem.at[src],
+            device_id={"expert": src},
+            device_id_type=MESH,
+        ).wait_recv()
+    left = jnp.concatenate([att_recv[i].astype(F32) for i in range(n_expert)], axis=0).astype(BF16)
+    proj_copies = []
+    tile = 512
+    for n in range(CHUNKS):
+        wo_copies[n].wait()
+
+        @pl.loop(0, chunk // tile)
+        def _(t):
+            cols = pl.ds(pl.multiple_of(n * chunk + t * tile, tile), tile)
+            product = jnp.dot(left, wo_buf[:, cols], preferred_element_type=F32)
+            for i in range(n_expert):
+                proj_own[i, :, cols] = product[i * rows : (i + 1) * rows]
+
+        cols = pl.ds(n * chunk, chunk)
+        for step in range(n_expert - 1):
+            dst = lax.rem(e + 1 + step, n_expert)
+            proj_send[n, step] = proj_own[dst, :, cols].astype(BF16)
+            copy = pltpu.make_async_remote_copy(
+                src_ref=proj_send.at[n, step],
+                dst_ref=proj_recv.at[n, step],
+                send_sem=proj_ssem.at[n, step],
+                recv_sem=proj_rsem.at[n, step],
+                device_id={"expert": dst},
+                device_id_type=MESH,
+            )
+            copy.start()
+            proj_copies.append(copy)
+    wd_copies = []
+    for j in range(local_experts):
+        wc = pltpu.make_async_copy(w_down.at[j], wo_buf.at[pl.ds(j * ff, ff), :], wd_sem.at[j])
+        wc.start()
+        wd_copies.append(wc)
+
+    squares = jnp.zeros((rows, 1), F32)
+    for n in range(CHUNKS):
+        cols = slice(n * chunk, (n + 1) * chunk)
+        total = residual[:, cols].astype(F32) + proj_own[e, :, cols]
+        for step in range(n_expert - 1):
+            proj_copies[n * (n_expert - 1) + step].wait_recv()
+            total = total + proj_recv[n, step].astype(F32)
+        total = total.astype(BF16).astype(F32)
+        hidden_buf[:, cols] = total
+        squares = squares + jnp.sum(total * total, axis=-1, keepdims=True)
+    inverse = lax.rsqrt(squares * (1.0 / width) + EPS)
+    for n in range(CHUNKS):
+        cols = slice(n * chunk, (n + 1) * chunk)
+        gathered[mine, :, cols] = (hidden_buf[:, cols] * inverse * norm_gain[:, cols]).astype(BF16)
+
+    def give(block, slot, device):
+        copy = pltpu.make_async_remote_copy(
+            src_ref=gathered.at[block],
+            dst_ref=gathered.at[block],
+            send_sem=gat_ssem.at[slot],
+            recv_sem=gat_rsem.at[block],
+            device_id=device,
+            device_id_type=MESH,
+        )
+        copy.start()
+        return copy
+
+    def arrive(block):
+        pltpu.make_async_remote_copy(
+            src_ref=gathered.at[block],
+            dst_ref=gathered.at[block],
+            send_sem=gat_ssem.at[0],
+            recv_sem=gat_rsem.at[block],
+            device_id={"expert": mate},
+            device_id_type=MESH,
+        ).wait_recv()
+
+    gives = []
+
+    def pass_on(block, device):
+        gives.append(give(block, len(gives), device))
+
+    pass_on(mine, {"expert": across})
+    for step in range(1, n_dp):
+        pass_on(mine, {"dp": lax.rem(z + step, n_dp)})
+    pass_on(mine, {"expert": mate})
+    for step in range(n_dp):
+        there = lax.rem(z + n_dp - step, n_dp)
+        if step:
+            block = e * n_dp + there
+            arrive(block)
+            pass_on(block, {"expert": across})
+            pass_on(block, {"expert": mate})
+        block = across * n_dp + there
+        arrive(block)
+        pass_on(block, {"expert": mate})
+    mate_across = lax.rem(mate + 2, 4)
+    for step in range(n_dp):
+        there = lax.rem(z + n_dp - step, n_dp)
+        arrive(mate * n_dp + there)
+        arrive(mate_across * n_dp + there)
+
+    blocks = n_expert * n_dp
+    all_rows = blocks * rows
+    for copy in gu_copies:
+        copy.wait()
+    all_weights = gathered[:, :, width:].astype(F32).reshape(all_rows, SIDE)
+    all_place = lax.broadcasted_iota(jnp.int32, (all_rows, SIDE), 1)
+
+    @pl.loop(0, local_experts)
+    def _(j):
+        cols = pl.ds(pl.multiple_of(j * (2 * ff), 2 * ff), 2 * ff)
+        total = jnp.zeros((all_rows, 2 * ff), F32)
+        for n in range(CHUNKS):
+            ks = slice(n * chunk, (n + 1) * chunk)
+            x = gathered[:, :, ks].reshape(all_rows, chunk)
+            total = total + jnp.dot(x, gu_buf[ks, cols], preferred_element_type=F32)
+        gate_out = total[:, :ff]
+        up_out = total[:, ff:]
+        column = jnp.sum(
+            jnp.where(all_place == e * local_experts + j, all_weights, 0.0), axis=-1, keepdims=True
+        )
+        activated = gate_out / (1.0 + jnp.exp(-gate_out)) * up_out * column
+        acts[:, pl.ds(pl.multiple_of(j * ff, ff), ff)] = activated.astype(BF16)
+
+    for copy in wd_copies:
+        copy.wait()
+
+    def stage(send, recv, ssem, rsem, device):
+        copy = pltpu.make_async_remote_copy(
+            src_ref=send, dst_ref=recv, send_sem=ssem, recv_sem=rsem, device_id=device, device_id_type=MESH
+        )
+        copy.start()
+        return copy
+
+    c1, c2, c3 = [], [], []
+
+    def down(n):
+        @pl.loop(0, chunk // tile)
+        def _(t):
+            cols = pl.ds(pl.multiple_of(n * chunk + t * tile, tile), tile)
+            here = pl.ds(pl.multiple_of(t * tile, tile), tile)
+            product = jnp.dot(
+                acts[...], wo_buf[: local_experts * ff, cols], preferred_element_type=F32
+            )
+            part[n, :, :, :, :, here] = product.reshape(2, 2, n_dp, rows, tile)
+
+        s1[n] = part[n, :, 1 - core].astype(BF16)
+        c1.append(stage(s1.at[n], r1.at[n], s1_sem.at[n], r1_sem.at[n], {"expert": mate}))
+
+    def second(n):
+        c1[n].wait_recv()
+        s2[n] = (part[n, 1 - y, core] + r1[n, 1 - y].astype(F32)).astype(BF16)
+        c2.append(stage(s2.at[n], r2.at[n], s2_sem.at[n], r2_sem.at[n], {"expert": across}))
+        part[n, y, core] = part[n, y, core] + r1[n, y].astype(F32)
+
+    def third(n):
+        c2[n].wait_recv()
+        for step in range(1, n_dp):
+            there = lax.rem(z + step, n_dp)
+            s3[n, step - 1] = (part[n, y, core, there] + r2[n, there].astype(F32)).astype(BF16)
+            c3.append(
+                stage(
+                    s3.at[n, step - 1],
+                    r3.at[n, step - 1],
+                    s3_sem.at[n, step - 1],
+                    r3_sem.at[n, step - 1],
+                    {"dp": there},
+                )
+            )
+
+    def finish(n):
+        cols = slice(n * chunk, (n + 1) * chunk)
+        total = part[n, y, core, z] + r2[n, z].astype(F32)
+        for step in range(n_dp - 1):
+            c3[n * (n_dp - 1) + step].wait_recv()
+            total = total + r3[n, step].astype(F32)
+        out[:, cols] = (hidden_buf[:, cols] + total).astype(BF16)
+
+    for n in range(CHUNKS + 2):
+        if n < CHUNKS:
+            down(n)
+        if 0 <= n - 1 < CHUNKS:
+            second(n - 1)
+        if 0 <= n - 2 < CHUNKS:
+            third(n - 2)
+    for n in range(CHUNKS):
+        finish(n)
+    for copy in att_copies + proj_copies + gives + c1 + c2 + c3:
+        copy.wait_send()
+
+
+def per_device_fused(sizes, *args):
+    n_expert, n_dp = sizes["expert"], sizes["dp"]
+    query, key_cache, w_gate = args[0], args[1], args[11]
+    residual, out_proj = args[6], args[7]
+    rows, kv_count, cache_len, head_size = key_cache.shape
+    width = residual.shape[1]
+    local_experts, _, ff = w_gate.shape
+    feat = out_proj.shape[0]
+    weight_bytes = 2 * (out_proj.size + 2 * w_gate.size + 2 * key_cache.size)
+    fits = (
+        n_expert == 4
+        and kv_count == n_expert
+        and ff % 128 == 0
+        and local_experts * ff <= feat
+        and rows == 8
+        and weight_bytes <= 48 * MIB
+    )
+    if not fits:
+        return per_device(*args)
+    per_group = query.shape[1] // (kv_count * head_size)
+    blocks = n_expert * n_dp
+    chunk = width // CHUNKS
+    dma = pltpu.SemaphoreType.DMA
+    vmem, anyspace = pl.BlockSpec(memory_space=pltpu.VMEM), pl.BlockSpec(memory_space=pl.ANY)
+    smem = pl.BlockSpec(memory_space=pltpu.SMEM)
+    specs = [vmem, anyspace, anyspace, vmem, vmem, smem, vmem, anyspace, vmem, vmem, vmem]
+    specs += [anyspace] * 3
+    operands = list(args)
+    operands[8] = args[8].reshape(1, width)
+    flops = 2 * blocks * rows * 3 * w_gate.size + 2 * n_expert * rows * out_proj.size
+    return pl.pallas_call(
+        functools.partial(fused_kernel, n_expert, n_dp),
+        out_shape=jax.ShapeDtypeStruct((rows, width), BF16),
+        in_specs=specs,
+        out_specs=vmem,
+        scratch_shapes=[
+            pltpu.VMEM((kv_count, rows, cache_len, head_size), BF16),
+            pltpu.VMEM((kv_count, rows, cache_len, head_size), BF16),
+            pltpu.VMEM((feat, width), BF16),
+            pltpu.VMEM((width, 2 * local_experts * ff), BF16),
+            pltpu.VMEM((rows * kv_count * per_group, head_size), F32),
+            pltpu.VMEM((rows * per_group, head_size), F32),
+            pltpu.VMEM((n_expert - 1, rows, feat), BF16),
+            pltpu.VMEM((n_expert, rows, feat), BF16),
+            pltpu.VMEM((CHUNKS, n_expert - 1, rows, chunk), BF16),
+            pltpu.VMEM((CHUNKS, n_expert - 1, rows, chunk), BF16),
+            pltpu.VMEM((n_expert, rows, width), F32),
+            pltpu.VMEM((rows, width), F32),
+            pltpu.VMEM((blocks, rows, width + SIDE), BF16),
+            pltpu.VMEM((blocks * rows, local_experts * ff), BF16),
+            pltpu.VMEM((CHUNKS, 2, 2, n_dp, rows, chunk), F32),
+            pltpu.VMEM((CHUNKS, 2, n_dp, rows, chunk), BF16),
+            pltpu.VMEM((CHUNKS, 2, n_dp, rows, chunk), BF16),
+            pltpu.VMEM((CHUNKS, n_dp, rows, chunk), BF16),
+            pltpu.VMEM((CHUNKS, n_dp, rows, chunk), BF16),
+            pltpu.VMEM((CHUNKS, n_dp - 1, rows, chunk), BF16),
+            pltpu.VMEM((CHUNKS, n_dp - 1, rows, chunk), BF16),
+            dma((2, n_expert)),
+            dma((CHUNKS,)),
+            dma((local_experts, 2)),
+            dma((local_experts,)),
+            dma((n_expert - 1,)),
+            dma((n_expert,)),
+            dma((CHUNKS, n_expert - 1)),
+            dma((CHUNKS, n_expert - 1)),
+            dma((4 * n_dp,)),
+            dma((blocks,)),
+            dma((CHUNKS,)),
+            dma((CHUNKS,)),
+            dma((CHUNKS,)),
+            dma((CHUNKS,)),
+            dma((CHUNKS, n_dp - 1)),
+            dma((CHUNKS, n_dp - 1)),
+        ],
+        compiler_params=pltpu.CompilerParams(
+            collective_id=0, has_side_effects=True, vmem_limit_bytes=60 * MIB
+        ),
+        cost_estimate=pl.CostEstimate(
+            flops=flops,
+            bytes_accessed=2 * (out_proj.size + 3 * w_gate.size + 2 * key_cache.size),
+            transcendentals=0,
+        ),
+    )(*operands)
+
+
 def solution(mesh):
     return jax.shard_map(
-        per_device,
+        functools.partial(per_device_fused, dict(mesh.shape)),
         mesh=mesh,
         in_specs=(
             P(("group", "expert", "dp"), None),

time: 185 us -> 61.9 us (0.33)
  waiting for transfers between devices: 89.4 us -> 0 us
  Pallas kernels: 0 us -> 60.3 us
  blocking collectives: 40.2 us -> 0 us
  matrix products: 35.4 us -> 0 us
  between operations: 13.2 us -> 0.01 us
  other arithmetic: 5.52 us -> 0 us
    reduce_scatter x2 -> x0, waiting for transfers between devices: 82.8 us -> none  [the longest x1 60.7 us: per_device(): lax.psum_scatter(jnp.dot(activated, down_flat, preferred_element_type=jnp...]
    pallas_call x0 -> x1, Pallas kernels: none -> 60.3 us  [per_device_fused(): pl.pallas_call(functools.partial(fused_kernel, n_expert, n_dp), out_shape...]
    dot_general x6 -> x0, matrix products: 35.4 us -> none  [the longest x1 13.4 us: per_device(): jnp.dot(activated, down_flat, preferred_element_type=jnp.float32)]
    all_gather x1 -> x0, blocking collectives: 31.5 us -> none  [per_device(): lax.all_gather(weighting, ('expert', 'dp'), axis=0, tiled=True)]
    all_to_all x1 -> x0, blocking collectives: 8.67 us -> none  [per_device(): lax.all_to_all(attended, 'expert', split_axis=1, concat_axis=0, tiled=True)]
    all_gather x1 -> x0, waiting for transfers between devices: 6.54 us -> none  [per_device(): lax.all_gather(normed, ('expert', 'dp'), axis=0, tiled=True)]
    convert_element_type x5 -> x0, other arithmetic: 2.3 us -> none  [the longest x1 1.55 us: per_device(): return (hidden_wide + expert_sum).astype(jnp.bfloat16)]
  transfers between devices with their start and end apart: 3 -> 0, of which waited for: 3 -> 0; matrix products, arithmetic and copies ran while one was open for 0% -> 0% of each run, Pallas kernels for 0% -> 0%
where the time goes in v1:
time: 61.9 us; the launch traced here: 61.7 us
  Pallas kernels  60.3 us (97%)
  local copies, waits for them, and re-layouts  1.47 us (2%)
    pallas_call x1, Pallas kernels, per_device_fused(): pl.pallas_call(functools.partial(fused_kernel, n_expert, n_dp), out_shape...  60.3 us
    unnamed x1, local copies, waits for them, and re-layouts  1.47 us

profile of v1, /device:TPU:0, one launch (start us, length us, event | category | flops | bytes accessed | tf_op | source)
XLA Modules:
  0.0 61.7 jit_solution(2589947951097059747)
XLA Ops:
  0.0 60.3 %shard_map.136 = bf16[8,4096]{1,0:T(8,128)(2,1)} custom-call(bf16[8,8192]{1,0:T(8,128)(2,1)} %query.1, bf16[8,4,256,128]{3,2,1,0:T(8,128)(2,1)} %key_cache.1, bf16[8,4,256,128]{3,2,1,0:T(8,128)(2,1)} %value_cache.1, bf16[8,512]{1,0:T(8,128)(2,1)} %new_key.1, bf16[8,512]{1,0:T(8,128)(2,1)} %new_value.1, s32[8]{0:T(128)} %lengths.1, bf16[8,4096]{1,0:T(8,128)(2,1)} %residual.1, ...), custom_call_target="tpu_custom_call" | custom-call | flops 5368709120 | bytes 58720256 | tf_op jit(solution)/shard_map/pallas_call | solution.py:520
  60.3 1.5 %copy.16 = bf16[8,4096]{1,0:T(8,128)(2,1)} copy(bf16[8,4096]{1,0:T(8,128)(2,1)} %shard_map.136) | data formatting | bytes 131072

commit v2 on v1

--- a/solution.py
+++ b/solution.py
@@ -150,6 +150,7 @@
     proj_own,
     hidden_buf,
     gathered,
+    gu_half,
     acts,
     part,
     s1,
@@ -181,6 +182,7 @@
     feat = att_send.shape[2]
     local_experts, _, ff = w_gate.shape
     chunk = width // CHUNKS
+    half = width // 2
     e = lax.axis_index("expert")
     z = lax.axis_index("dp")
     core = lax.rem(e, 2)
@@ -290,7 +292,8 @@
     for t in range(ids.shape[1]):
         weighting = weighting + jnp.where(side_place == ids[:, t : t + 1], probs[:, t : t + 1], 0.0)
     mine = e * n_dp + z
-    gathered[mine, :, width:] = weighting.astype(BF16)
+    gathered[0, mine, :, half:] = weighting.astype(BF16)
+    gathered[1, mine, :, half:] = jnp.zeros((rows, SIDE), BF16)
 
     for step in range(n_expert - 1):
         src = lax.rem(e + 1 + step, n_expert)
@@ -346,72 +349,95 @@
         hidden_buf[:, cols] = total
         squares = squares + jnp.sum(total * total, axis=-1, keepdims=True)
     inverse = lax.rsqrt(squares * (1.0 / width) + EPS)
-    for n in range(CHUNKS):
-        cols = slice(n * chunk, (n + 1) * chunk)
-        gathered[mine, :, cols] = (hidden_buf[:, cols] * inverse * norm_gain[:, cols]).astype(BF16)
-
-    def give(block, slot, device):
+    def give(part_no, block, slot, device):
         copy = pltpu.make_async_remote_copy(
-            src_ref=gathered.at[block],
-            dst_ref=gathered.at[block],
+            src_ref=gathered.at[part_no, block],
+            dst_ref=gathered.at[part_no, block],
             send_sem=gat_ssem.at[slot],
-            recv_sem=gat_rsem.at[block],
+            recv_sem=gat_rsem.at[part_no, block],
             device_id=device,
             device_id_type=MESH,
         )
         copy.start()
         return copy
 
-    def arrive(block):
+    def arrive(part_no, block):
         pltpu.make_async_remote_copy(
-            src_ref=gathered.at[block],
-            dst_ref=gathered.at[block],
+            src_ref=gathered.at[part_no, block],
+            dst_ref=gathered.at[part_no, block],
             send_sem=gat_ssem.at[0],
-            recv_sem=gat_rsem.at[block],
+            recv_sem=gat_rsem.at[part_no, block],
             device_id={"expert": mate},
             device_id_type=MESH,
         ).wait_recv()
 
     gives = []
 
-    def pass_on(block, device):
-        gives.append(give(block, len(gives), device))
-
-    pass_on(mine, {"expert": across})
-    for step in range(1, n_dp):
-        pass_on(mine, {"dp": lax.rem(z + step, n_dp)})
-    pass_on(mine, {"expert": mate})
-    for step in range(n_dp):
+    def pass_on(part_no, block, device):
+        gives.append(give(part_no, block, len(gives), device))
+
+    def begin(part_no):
+        start = part_no * half
+        gathered[part_no, mine, :, :half] = (
+            hidden_buf[:, start : start + half] * inverse * norm_gain[:, start : start + half]
+        ).astype(BF16)
+        pass_on(part_no, mine, {"expert": across})
+        for step in range(1, n_dp):
+            pass_on(part_no, mine, {"dp": lax.rem(z + step, n_dp)})
+        pass_on(part_no, mine, {"expert": mate})
+
+    def forward(part_no, step):
         there = lax.rem(z + n_dp - step, n_dp)
         if step:
             block = e * n_dp + there
-            arrive(block)
-            pass_on(block, {"expert": across})
-            pass_on(block, {"expert": mate})
+            arrive(part_no, block)
+            pass_on(part_no, block, {"expert": across})
+            pass_on(part_no, block, {"expert": mate})
         block = across * n_dp + there
-        arrive(block)
-        pass_on(block, {"expert": mate})
+        arrive(part_no, block)
+        pass_on(part_no, block, {"expert": mate})
+
     mate_across = lax.rem(mate + 2, 4)
+
+    def complete(part_no):
+        for step in range(n_dp):
+            there = lax.rem(z + n_dp - step, n_dp)
+            arrive(part_no, mate * n_dp + there)
+            arrive(part_no, mate_across * n_dp + there)
+
+    begin(0)
+    begin(1)
     for step in range(n_dp):
-        there = lax.rem(z + n_dp - step, n_dp)
-        arrive(mate * n_dp + there)
-        arrive(mate_across * n_dp + there)
+        forward(0, step)
+    complete(0)
 
     blocks = n_expert * n_dp
     all_rows = blocks * rows
-    for copy in gu_copies:
-        copy.wait()
-    all_weights = gathered[:, :, width:].astype(F32).reshape(all_rows, SIDE)
+    all_weights = gathered[0, :, :, half:].astype(F32).reshape(all_rows, SIDE)
     all_place = lax.broadcasted_iota(jnp.int32, (all_rows, SIDE), 1)
+
+    def half_product(part_no, cols):
+        total = jnp.zeros((all_rows, 2 * ff), F32)
+        for n in range(CHUNKS // 2):
+            x = gathered[part_no, :, :, n * chunk : (n + 1) * chunk].reshape(all_rows, chunk)
+            first = part_no * half + n * chunk
+            total = total + jnp.dot(x, gu_buf[first : first + chunk, cols], preferred_element_type=F32)
+        return total
+
+    for step in range(max(local_experts, n_dp)):
+        if step < local_experts:
+            gu_copies[2 * step].wait()
+            gu_copies[2 * step + 1].wait()
+            cols = slice(step * 2 * ff, (step + 1) * 2 * ff)
+            gu_half[:, cols] = half_product(0, cols)
+        if step < n_dp:
+            forward(1, step)
+    complete(1)
 
     @pl.loop(0, local_experts)
     def _(j):
         cols = pl.ds(pl.multiple_of(j * (2 * ff), 2 * ff), 2 * ff)
-        total = jnp.zeros((all_rows, 2 * ff), F32)
-        for n in range(CHUNKS):
-            ks = slice(n * chunk, (n + 1) * chunk)
-            x = gathered[:, :, ks].reshape(all_rows, chunk)
-            total = total + jnp.dot(x, gu_buf[ks, cols], preferred_element_type=F32)
+        total = gu_half[:, cols] + half_product(1, cols)
         gate_out = total[:, :ff]
         up_out = total[:, ff:]
         column = jnp.sum(
@@ -535,7 +561,8 @@
             pltpu.VMEM((CHUNKS, n_expert - 1, rows, chunk), BF16),
             pltpu.VMEM((n_expert, rows, width), F32),
             pltpu.VMEM((rows, width), F32),
-            pltpu.VMEM((blocks, rows, width + SIDE), BF16),
+            pltpu.VMEM((2, blocks, rows, width // 2 + SIDE), BF16),
+            pltpu.VMEM((blocks * rows, 2 * local_experts * ff), F32),
             pltpu.VMEM((blocks * rows, local_experts * ff), BF16),
             pltpu.VMEM((CHUNKS, 2, 2, n_dp, rows, chunk), F32),
             pltpu.VMEM((CHUNKS, 2, n_dp, rows, chunk), BF16),
@@ -552,8 +579,8 @@
             dma((n_expert,)),
             dma((CHUNKS, n_expert - 1)),
             dma((CHUNKS, n_expert - 1)),
-            dma((4 * n_dp,)),
-            dma((blocks,)),
+            dma((8 * n_dp,)),
+            dma((2, blocks)),
             dma((CHUNKS,)),
             dma((CHUNKS,)),
             dma((CHUNKS,)),

time: 61.9 us -> 69.9 us (1.13)
  Pallas kernels: 60.3 us -> 68.2 us
    pallas_call x1, Pallas kernels: 60.3 us -> 68.2 us  [per_device_fused(): pl.pallas_call(functools.partial(fused_kernel, n_expert, n_dp), out_shape...]
where the time goes in v2:
time: 69.9 us; the launch traced here: 69.7 us
  Pallas kernels  68.2 us (98%)
  local copies, waits for them, and re-layouts  1.47 us (2%)
    pallas_call x1, Pallas kernels, per_device_fused(): pl.pallas_call(functools.partial(fused_kernel, n_expert, n_dp), out_shape...  68.2 us
    unnamed x1, local copies, waits for them, and re-layouts  1.47 us

profile of v2, /device:TPU:0, one launch (start us, length us, event | category | flops | bytes accessed | tf_op | source)
XLA Modules:
  0.0 69.7 jit_solution(687656299776398087)
XLA Ops:
  0.0 68.2 %shard_map.136 = bf16[8,4096]{1,0:T(8,128)(2,1)} custom-call(bf16[8,8192]{1,0:T(8,128)(2,1)} %query.1, bf16[8,4,256,128]{3,2,1,0:T(8,128)(2,1)} %key_cache.1, bf16[8,4,256,128]{3,2,1,0:T(8,128)(2,1)} %value_cache.1, bf16[8,512]{1,0:T(8,128)(2,1)} %new_key.1, bf16[8,512]{1,0:T(8,128)(2,1)} %new_value.1, s32[8]{0:T(128)} %lengths.1, bf16[8,4096]{1,0:T(8,128)(2,1)} %residual.1, ...), custom_call_target="tpu_custom_call" | custom-call | flops 5368709120 | bytes 58720256 | tf_op jit(solution)/shard_map/pallas_call | solution.py:546
  68.2 1.5 %copy.16 = bf16[8,4096]{1,0:T(8,128)(2,1)} copy(bf16[8,4096]{1,0:T(8,128)(2,1)} %shard_map.136) | data formatting | bytes 131072

commit v3 on v1

--- a/solution.py
+++ b/solution.py
@@ -350,50 +350,74 @@
         cols = slice(n * chunk, (n + 1) * chunk)
         gathered[mine, :, cols] = (hidden_buf[:, cols] * inverse * norm_gain[:, cols]).astype(BF16)
 
-    def give(block, slot, device):
-        copy = pltpu.make_async_remote_copy(
+    def carry(block, kind, slot, device):
+        return pltpu.make_async_remote_copy(
             src_ref=gathered.at[block],
             dst_ref=gathered.at[block],
-            send_sem=gat_ssem.at[slot],
+            send_sem=gat_ssem.at[kind, slot],
             recv_sem=gat_rsem.at[block],
             device_id=device,
             device_id_type=MESH,
         )
-        copy.start()
-        return copy
 
     def arrive(block):
-        pltpu.make_async_remote_copy(
-            src_ref=gathered.at[block],
-            dst_ref=gathered.at[block],
-            send_sem=gat_ssem.at[0],
-            recv_sem=gat_rsem.at[block],
-            device_id={"expert": mate},
-            device_id_type=MESH,
-        ).wait_recv()
-
-    gives = []
-
-    def pass_on(block, device):
-        gives.append(give(block, len(gives), device))
-
-    pass_on(mine, {"expert": across})
-    for step in range(1, n_dp):
-        pass_on(mine, {"dp": lax.rem(z + step, n_dp)})
-    pass_on(mine, {"expert": mate})
-    for step in range(n_dp):
-        there = lax.rem(z + n_dp - step, n_dp)
-        if step:
+        carry(block, 0, 0, {"expert": mate}).wait_recv()
+
+    right, left_dp = {"dp": z + 1}, {"dp": z - 1}
+    has_right, has_left = z + 1 < n_dp, z > 0
+    other, partner = {"expert": across}, {"expert": mate}
+
+    @pl.when(has_right)
+    def _():
+        carry(mine, 0, 0, right).start()
+
+    @pl.when(has_left)
+    def _():
+        carry(mine, 1, 0, left_dp).start()
+
+    carry(mine, 2, 0, other).start()
+    carry(mine, 4, 0, partner).start()
+
+    def from_side(step, sign):
+        kind = 0 if sign < 0 else 1
+        there = z + sign * step
+        inside = there >= 0 if sign < 0 else there < n_dp
+        onward = has_right if sign < 0 else has_left
+        target = right if sign < 0 else left_dp
+
+        @pl.when(inside)
+        def _():
             block = e * n_dp + there
             arrive(block)
-            pass_on(block, {"expert": across})
-            pass_on(block, {"expert": mate})
-        block = across * n_dp + there
-        arrive(block)
-        pass_on(block, {"expert": mate})
+
+            @pl.when(onward)
+            def _():
+                carry(block, kind, step, target).start()
+
+            carry(block, 2 + kind, step, other).start()
+            carry(block, 4 + kind, step, partner).start()
+
+    def from_across(step, sign):
+        kind = 0 if sign < 0 else 1
+        there = z + sign * step
+        inside = there >= 0 if sign < 0 else there < n_dp
+
+        @pl.when(inside)
+        def _():
+            block = across * n_dp + there
+            arrive(block)
+            carry(block, 6 + kind, step, partner).start()
+
+    for step in range(1, n_dp):
+        from_side(step, -1)
+        from_side(step, 1)
+        from_across(step - 1, -1)
+        if step > 1:
+            from_across(step - 1, 1)
+    from_across(n_dp - 1, -1)
+    from_across(n_dp - 1, 1)
     mate_across = lax.rem(mate + 2, 4)
-    for step in range(n_dp):
-        there = lax.rem(z + n_dp - step, n_dp)
+    for there in range(n_dp):
         arrive(mate * n_dp + there)
         arrive(mate_across * n_dp + there)
 
@@ -483,8 +507,29 @@
             third(n - 2)
     for n in range(CHUNKS):
         finish(n)
-    for copy in att_copies + proj_copies + gives + c1 + c2 + c3:
+    for copy in att_copies + proj_copies + c1 + c2 + c3:
         copy.wait_send()
+
+    def drain(step, sign):
+        kind = 0 if sign < 0 else 1
+        there = z + sign * step
+        inside = there >= 0 if sign < 0 else there < n_dp
+        onward = has_right if sign < 0 else has_left
+
+        @pl.when(inside)
+        def _():
+            @pl.when(onward)
+            def _():
+                carry(e * n_dp + there, kind, step, partner).wait_send()
+
+            if step or sign < 0:
+                carry(e * n_dp + there, 2 + kind, step, partner).wait_send()
+                carry(e * n_dp + there, 4 + kind, step, partner).wait_send()
+                carry(across * n_dp + there, 6 + kind, step, partner).wait_send()
+
+    for step in range(n_dp):
+        drain(step, -1)
+        drain(step, 1)
 
 
 def per_device_fused(sizes, *args):
@@ -552,7 +597,7 @@
             dma((n_expert,)),
             dma((CHUNKS, n_expert - 1)),
             dma((CHUNKS, n_expert - 1)),
-            dma((4 * n_dp,)),
+            dma((8, n_dp)),
             dma((blocks,)),
             dma((CHUNKS,)),
             dma((CHUNKS,)),

time: 61.9 us -> 58.3 us (0.942)
  Pallas kernels: 60.3 us -> 56.6 us
    pallas_call x1, Pallas kernels: 60.3 us -> 56.6 us  [per_device_fused(): pl.pallas_call(functools.partial(fused_kernel, n_expert, n_dp), out_shape...]
where the time goes in v3:
time: 58.3 us; the launch traced here: 58.1 us
  Pallas kernels  56.6 us (97%)
  local copies, waits for them, and re-layouts  1.47 us (3%)
    pallas_call x1, Pallas kernels, per_device_fused(): pl.pallas_call(functools.partial(fused_kernel, n_expert, n_dp), out_shape...  56.6 us
    unnamed x1, local copies, waits for them, and re-layouts  1.47 us

profile of v3, /device:TPU:0, one launch (start us, length us, event | category | flops | bytes accessed | tf_op | source)
XLA Modules:
  0.0 58.1 jit_solution(14815085687307950056)
XLA Ops:
  0.0 56.6 %shard_map.136 = bf16[8,4096]{1,0:T(8,128)(2,1)} custom-call(bf16[8,8192]{1,0:T(8,128)(2,1)} %query.1, bf16[8,4,256,128]{3,2,1,0:T(8,128)(2,1)} %key_cache.1, bf16[8,4,256,128]{3,2,1,0:T(8,128)(2,1)} %value_cache.1, bf16[8,512]{1,0:T(8,128)(2,1)} %new_key.1, bf16[8,512]{1,0:T(8,128)(2,1)} %new_value.1, s32[8]{0:T(128)} %lengths.1, bf16[8,4096]{1,0:T(8,128)(2,1)} %residual.1, ...), custom_call_target="tpu_custom_call" | custom-call | flops 5368709120 | bytes 58720256 | tf_op jit(solution)/shard_map/pallas_call | solution.py:565
  56.6 1.5 %copy.16 = bf16[8,4096]{1,0:T(8,128)(2,1)} copy(bf16[8,4096]{1,0:T(8,128)(2,1)} %shard_map.136) | data formatting | bytes 131072

commit v4 on v3

--- a/solution.py
+++ b/solution.py
@@ -218,7 +218,6 @@
             gc = pltpu.make_async_copy(
                 w.at[j], gu_buf.at[:, pl.ds((2 * j + t) * ff, ff)], gu_sem.at[j, t]
             )
-            gc.start()
             gu_copies.append(gc)
 
     for h in range(kv_count * per_group):
@@ -281,6 +280,9 @@
             )
             copy.start()
             att_copies.append(copy)
+
+    for copy in gu_copies:
+        copy.start()
 
     probs = gate_probs[...]
     probs = probs / jnp.sum(probs, axis=-1, keepdims=True)

time: 58.3 us -> 54.2 us (0.930)
  Pallas kernels: 56.6 us -> 52.5 us
    pallas_call x1, Pallas kernels: 56.6 us -> 52.5 us  [per_device_fused(): pl.pallas_call(functools.partial(fused_kernel, n_expert, n_dp), out_shape...]
where the time goes in v4:
time: 54.2 us; the launch traced here: 54 us
  Pallas kernels  52.5 us (97%)
  local copies, waits for them, and re-layouts  1.47 us (3%)
    pallas_call x1, Pallas kernels, per_device_fused(): pl.pallas_call(functools.partial(fused_kernel, n_expert, n_dp), out_shape...  52.5 us
    unnamed x1, local copies, waits for them, and re-layouts  1.47 us

profile of v4, /device:TPU:0, one launch (start us, length us, event | category | flops | bytes accessed | tf_op | source)
XLA Modules:
  0.0 54.0 jit_solution(3260303806638549577)
XLA Ops:
  0.0 52.5 %shard_map.136 = bf16[8,4096]{1,0:T(8,128)(2,1)} custom-call(bf16[8,8192]{1,0:T(8,128)(2,1)} %query.1, bf16[8,4,256,128]{3,2,1,0:T(8,128)(2,1)} %key_cache.1, bf16[8,4,256,128]{3,2,1,0:T(8,128)(2,1)} %value_cache.1, bf16[8,512]{1,0:T(8,128)(2,1)} %new_key.1, bf16[8,512]{1,0:T(8,128)(2,1)} %new_value.1, s32[8]{0:T(128)} %lengths.1, bf16[8,4096]{1,0:T(8,128)(2,1)} %residual.1, ...), custom_call_target="tpu_custom_call" | custom-call | flops 5368709120 | bytes 58720256 | tf_op jit(solution)/shard_map/pallas_call | solution.py:567
  52.6 1.5 %copy.16 = bf16[8,4096]{1,0:T(8,128)(2,1)} copy(bf16[8,4096]{1,0:T(8,128)(2,1)} %shard_map.136) | data formatting | bytes 131072
